TPU v7x, 128 devices: a whole 4x4x4 slice. The times are simulated.
128 devices in a mesh: expert: 8 (over x_lo, z), tensor: 16 (over x_hi, y, core).
Axes of the slice: x: 4 (x_hi: 2, x_lo: 2; x = x_hi * 2 + x_lo), y: 4, z: 4, core: 2. Of those that a mesh axis runs over, the one named last changes fastest.
Arguments:
- tokens: bfloat16 [1024, 7168], P(('expert', 'tensor')), may hold values from -6 to 6
- route_ids: int32 [1024, 2], P(('expert', 'tensor')), may hold values from 0 to 7, all different within a row; in each aligned block of 128 rows (0 to 127, 128 to 255, ...) at most 64 rows name the same one
- route_gain: int32 [1024, 2], P(('expert', 'tensor')), may hold values from 1 to 1023
- norm_gain: float32 [7168], replicated, may hold values from 0.1 to 1.9
- dense_gate: bfloat16 [7168, 4864], P(None, 'tensor'), may hold values from -0.0625 to 0.0625
- dense_up: bfloat16 [7168, 4864], P(None, 'tensor'), may hold values from -0.0625 to 0.0625
- dense_down: bfloat16 [4864, 7168], P('tensor'), may hold values from -0.078125 to 0.078125
- expert_gate: bfloat16 [8, 7168, 4864], P('expert', None, 'tensor'), may hold values from -0.0625 to 0.0625
- expert_up: bfloat16 [8, 7168, 4864], P('expert', None, 'tensor'), may hold values from -0.0625 to 0.0625
- expert_down: bfloat16 [8, 4864, 7168], P('expert', 'tensor'), may hold values from -0.078125 to 0.078125
Outputs:
- mixed: bfloat16 [1024, 7168], P(('expert', 'tensor'))
Inputs may be any that keep to these rules, and one draw needn't show every extreme that they name: route_ids names two different experts for every token; in each aligned block of 128 rows no expert is named more than 64 times, a bound that some block reaches.
All inputs are finite; a program needn't handle non-finite values.
Results may differ from a plain program's by a relative error of at most 0.015.
Values may be sent and summed in bfloat16 or wider, within the bound.
A program may use at most 128 MiB of HBM per device.

v0:
```python
import jax
import jax.numpy as jnp
from jax import lax
from jax.sharding import PartitionSpec as P


def per_device(
    tokens,
    route_ids,
    route_gain,
    norm_gain,
    dense_gate,
    dense_up,
    dense_down,
    expert_gate,
    expert_up,
    expert_down,
):
    rows_all, ids_all, gains_all = (
        lax.all_gather(tokens, "tensor", axis=0, tiled=True),
        lax.all_gather(route_ids, "tensor", axis=0, tiled=True),
        lax.all_gather(route_gain, "tensor", axis=0, tiled=True),
    )
    group_rows = rows_all.shape[0]
    row_width = rows_all.shape[1]
    local_count = expert_gate.shape[0]
    expert_devices = lax.axis_size("expert")
    experts = expert_devices * local_count
    capacity = 4 * group_rows // experts
    floats = rows_all.astype(jnp.float32)
    normed = (
        floats * lax.rsqrt(jnp.mean(floats * floats, axis=1, keepdims=True) + 1e-05) * norm_gain
    ).astype(jnp.bfloat16)
    gate_vals = jnp.dot(normed, dense_gate, preferred_element_type=jnp.float32)
    up_vals = jnp.dot(normed, dense_up, preferred_element_type=jnp.float32)
    dense_hidden = (jax.nn.silu(gate_vals) * up_vals).astype(jnp.bfloat16)
    dense_part = jnp.dot(dense_hidden, dense_down, preferred_element_type=jnp.float32)
    flat_ids = ids_all.reshape(-1)
    onehot = (flat_ids[:, None] == jnp.arange(experts, dtype=jnp.int32)[None, :]).astype(jnp.int32)
    slot_rank = jnp.sum(onehot * (jnp.cumsum(onehot, axis=0) - 1), axis=1)
    source_row = jnp.arange(flat_ids.shape[0], dtype=jnp.int32) // 2
    outgoing = (
        jnp.zeros((experts, capacity, row_width), jnp.bfloat16)
        .at[flat_ids, slot_rank]
        .set(normed[source_row])
    )
    outgoing = outgoing.reshape(expert_devices, local_count, capacity, row_width)
    received = lax.all_to_all(outgoing, "expert", split_axis=0, concat_axis=0, tiled=True)
    gate_e = jnp.einsum("sxcd,xdf->sxcf", received, expert_gate, preferred_element_type=jnp.float32)
    up_e = jnp.einsum("sxcd,xdf->sxcf", received, expert_up, preferred_element_type=jnp.float32)
    hidden_e = (jax.nn.silu(gate_e) * up_e).astype(jnp.bfloat16)
    back = lax.all_to_all(
        jnp.einsum(
            "sxcf,xfd->sxcd", hidden_e, expert_down, preferred_element_type=jnp.float32
        ).astype(jnp.bfloat16),
        "expert",
        split_axis=0,
        concat_axis=0,
        tiled=True,
    )
    back = back.reshape(experts, capacity, back.shape[3])
    picked = back[flat_ids, slot_rank].astype(jnp.float32).reshape(group_rows, 2, back.shape[2])
    route_weight = gains_all.astype(jnp.float32) / 1024.0
    expert_sum = jnp.sum(picked * route_weight[:, :, None], axis=1)
    summed_rows = lax.psum_scatter(
        (dense_part + expert_sum).astype(jnp.bfloat16), "tensor", scatter_dimension=0, tiled=True
    ).astype(jnp.float32)
    return (tokens.astype(jnp.float32) + summed_rows).astype(jnp.bfloat16)


def solution(mesh):
    return jax.shard_map(
        per_device,
        mesh=mesh,
        in_specs=(
            P(("expert", "tensor"), None),
            P(("expert", "tensor"), None),
            P(("expert", "tensor"), None),
            P(),
            P(None, "tensor"),
            P(None, "tensor"),
            P("tensor", None),
            P("expert", None, "tensor"),
            P("expert", None, "tensor"),
            P("expert", "tensor", None),
        ),
        out_specs=P(("expert", "tensor"), None),
        check_vma=False,
    )
```

profile of v0, /device:TPU:1, one launch (start us, length us, event | category | flops | bytes accessed | tf_op | source)
XLA Modules:
  0.0 501.2 jit_solution(14148694152243159261)
XLA Ops:
  6.5 0.0 all-gather.4.cloned.1.call-start
  6.5 0.7 all-gather.4.cloned.1.call-update
  7.3 26.0 %all-gather = s32[16,8,2]{1,2,0:T(2,128)S(1)} all-gather(s32[1,8,2]{1,2,0:T(2,128)} %bitcast.98), channel_id=1, replica_groups=mesh['expert'=8,'tensor'=16] {'tensor'}, dimensions={0}, use_global_device_ids=true | all-gather | bytes 1088 | tf_op jit(solution)/shard_map/all_gather | solution.py:21
  33.2 0.2 copy.22
  33.4 0.1 eq.29
  33.5 0.1 eq.25
  33.7 0.1 reshape.146
  33.8 0.6 reduce-window.6
  34.4 0.2 slice_reduce_fusion
  34.7 0.1 fusion.49
  34.8 25.3 %all-gather.4.cloned.1.call-done = bf16[128,7168]{1,0:T(8,128)(2,1)} async-done(((bf16[8,7168]{1,0:T(8,128)(2,1)}), bf16[128,7168]{1,0:T(8,128)(2,1)}) %all-gather.4.cloned.1.call-update) | async-done | bytes 1835024 | tf_op jit(solution)/shard_map/all_gather | solution.py:20
  60.2 1.9 fusion.9
  62.1 2.0 fusion.11
  64.1 4.8 gather_fusion
  68.9 3.9 broadcast_in_dim.2
  72.8 95.6 %scatter_fusion = bf16[8,64,7168]{2,1,0:T(8,128)(2,1)} fusion(bf16[8,64,7168]{2,1,0:T(8,128)(2,1)} %broadcast_in_dim.2, s32[256]{0:T(256)S(1)} %bitcast.95, bf16[256,7168]{1,0:T(8,128)(2,1)} %gather_fusion), kind=kCustom, calls=%fused_computation.2 | custom fusion | bytes 11012096 | tf_op jit(solution)/shard_map/scatter | solution.py:45
  168.3 86.7 %all_to_all.10 = bf16[8,1,64,7168]{3,2,1,0:T(8,128)(2,1)S(1)} all-to-all(bf16[8,1,64,7168]{3,2,1,0:T(8,128)(2,1)} %bitcast.93), channel_id=1, replica_groups=mesh['expert'=8,'tensor'=16] {'expert'}, dimensions={0} | all-to-all | bytes 14680064 | tf_op jit(solution)/shard_map/all_to_all | solution.py:48
  255.1 0.0 copy-start
  255.1 3.0 copy-done
  258.0 6.2 %fusion.12 = f32[8,1,64,304]{3,2,0,1:T(8,128)S(1)} fusion(bf16[1,7168,304]{1,2,0:T(8,128)(2,1)} %param.17, bf16[8,1,64,7168]{3,2,1,0:T(8,128)(2,1)S(1)} %all_to_all.10), kind=kOutput, calls=%fused_computation.20 | convolution fusion | flops 2231369728 | bytes 12320768 | tf_op jit(solution)/shard_map/sxcd,xdf->sxcf/dot_general | solution.py:49
  264.2 14.8 %fusion = bf16[8,1,64,7168]{3,2,1,0:T(8,128)(2,1)} fusion(bf16[1,304,7168]{2,1,0:T(8,128)(2,1)} %param.19, bf16[1,7168,304]{1,2,0:T(8,128)(2,1)} %param.18, bf16[8,1,64,7168]{3,2,1,0:T(8,128)(2,1)} %copy-done, f32[8,1,64,304]{3,2,0,1:T(8,128)S(1)} %fusion.12), kind=kOutput, calls=%fused_computation.4 | convolution fusion | flops 4467343360 | bytes 24018944 | tf_op jit(solution)/shard_map/sxcf,xfd->sxcd/dot_general | solution.py:53
  279.0 0.0 copy-start.2
  279.0 5.0 all-to-all-start.1
  284.0 0.0 reduce-scatter.2.cloned.1.call-start
  284.1 0.0 copy-done.2
  284.1 96.7 %all-gather.1 = s32[16,8,2]{1,2,0:T(2,128)S(1)} all-gather(s32[1,8,2]{1,2,0:T(2,128)S(1)} %bitcast.99), channel_id=1, replica_groups=mesh['expert'=8,'tensor'=16] {'tensor'}, dimensions={0}, use_global_device_ids=true | all-gather | bytes 1088 | tf_op jit(solution)/shard_map/all_gather | solution.py:22
  380.8 0.1 copy.26
  380.9 0.1 copy.29
  381.0 3.5 fusion.55
  384.5 0.0 all-to-all-done.1
  384.5 11.2 %gather_fusion.1 = bf16[256,7168]{1,0:T(8,128)(2,1)} fusion(bf16[8,64,7168]{2,1,0:T(8,128)(2,1)} %bitcast.27, s32[256]{0:T(256)S(1)} %bitcast.94), kind=kCustom, calls=%fused_computation.1 | custom fusion | bytes 7342080 | tf_op jit(solution)/shard_map/gather | solution.py:62
  395.7 8.6 %reshape.155 = f32[128,2,7168]{2,1,0:T(2,128)} reshape(bf16[256,7168]{1,0:T(8,128)(2,1)} %gather_fusion.1) | data formatting | bytes 11010048 | tf_op jit(solution)/shard_map/convert_element_type | solution.py:62
  404.3 12.9 %multiply_reduce_fusion = f32[128,7168]{1,0:T(8,128)} fusion(f32[128,2,7168]{2,1,0:T(2,128)} %reshape.155, f32[128,2]{1,0:T(8,128)S(1)} %bitcast.96), kind=kLoop, calls=%fused_computation.11 | loop fusion | flops 2752512 | bytes 11011072 | tf_op jit(solution)/shard_map/reduce_sum | solution.py:64
  417.2 0.0 copy-start.1
  417.2 10.2 %fusion.1 = bf16[128,7168]{1,0:T(8,128)(2,1)} fusion(f32[128,7168]{1,0:T(8,128)} %multiply_reduce_fusion, bf16[304,7168]{1,0:T(8,128)(2,1)} %param.16, bf16[128,7168]{1,0:T(8,128)(2,1)S(1)} %fusion.11, bf16[7168,304]{0,1:T(8,128)(2,1)} %param.15, f32[128,304]{0,1:T(8,128)S(1)} %fusion.55), kind=kOutput, calls=%fused_computation.6 | convolution fusion | flops 1117753344 | bytes 16211968 | tf_op jit(solution)/shard_map/dot_general | solution.py:37
  427.4 0.0 reduce-scatter.2.cloned.1.call-update
  427.4 65.4 %reduce-scatter.2.cloned.1.call-done = bf16[8,7168]{1,0:T(8,128)(2,1)} async-done(((bf16[128,7168]{1,0:T(8,128)(2,1)}), bf16[8,7168]{1,0:T(8,128)(2,1)}) %reduce-scatter.2.cloned.1.call-update) | async-done | bytes 114704 | tf_op jit(solution)/shard_map/reduce_scatter | solution.py:65
  492.8 0.0 copy-done.1
  492.8 1.6 add_convert_fusion
  (8 shorter events, 0.1 us)
Async XLA Ops:
  6.5 53.6 %all-gather.4.cloned.1.call-start = ((), (), s32[]{:S(2)}) async-start(), calls=%async_computation.3 | async-start | bytes 1949696 | tf_op jit(solution)/shard_map/all_gather | solution.py:20
  255.1 3.0 copy-start
  279.0 5.0 %copy-start.2 = (s32[8,2]{0,1:T(2,128)S(1)}, s32[8,2]{0,1:T(2,128)}, u32[]{:S(2)}) copy-start(s32[8,2]{0,1:T(2,128)} %param.12) | copy-start | bytes 196
  279.0 105.5 %all-to-all-start.1 = ((bf16[8,1,64,7168]{3,2,1,0:T(8,128)(2,1)}), bf16[8,1,64,7168]{3,2,1,0:T(8,128)(2,1)}, u32[]{:S(2)}, u32[]{:S(2)}) async-start(bf16[8,1,64,7168]{3,2,1,0:T(8,128)(2,1)} %fusion), calls=%async_computation.1 | async-start | bytes 14680064 | tf_op jit(solution)/shard_map/all_to_all | solution.py:52
  284.0 208.8 %reduce-scatter.2.cloned.1.call-start = ((), (), s32[]{:S(2)}) async-start(), calls=%async_computation.4 | async-start | bytes 1949696 | tf_op jit(solution)/shard_map/reduce_scatter | solution.py:65
  417.2 75.6 %copy-start.1 = (bf16[8,7168]{1,0:T(8,128)(2,1)S(1)}, bf16[8,7168]{1,0:T(8,128)(2,1)}, u32[]{:S(2)}) copy-start(bf16[8,7168]{1,0:T(8,128)(2,1)} %param.10) | copy-start | bytes 344068
Sparse Core Ops, SparseCore 0:
  9.8 50.2 all-gather.3
  427.5 65.2 reduce-scatter.1
where the time goes:
time: 503 us; the launch traced here: 501 us
  blocking collectives  209 us (42%)
  local copies, waits for them, and re-layouts  128 us (25%)
  waiting for transfers between devices  91.5 us (18%)
  matrix products  34.7 us (7%)
  other arithmetic  19.2 us (4%)
  between operations  13.5 us (3%)
    all_gather x1, blocking collectives, per_device(): lax.all_gather(route_gain, 'tensor', axis=0, tiled=True)  96.7 us
    scatter x1, local copies, waits for them, and re-layouts, per_device(): outgoing = jnp.zeros((experts, capacity, row_width), jnp.bfloat16).at[fla...  95.6 us
    all_to_all x1, blocking collectives, per_device(): lax.all_to_all(outgoing, 'expert', split_axis=0, concat_axis=0, tiled=True)  86.7 us
    reduce_scatter x1, waiting for transfers between devices, per_device(): lax.psum_scatter((dense_part + expert_sum).astype(jnp.bfloat16), 'tensor'...  65.4 us
    all_gather x1, blocking collectives, per_device(): lax.all_gather(route_ids, 'tensor', axis=0, tiled=True)  26 us
    all_gather x1, waiting for transfers between devices, per_device(): lax.all_gather(tokens, 'tensor', axis=0, tiled=True)  25.3 us
    dot_general x1, matrix products, per_device(): jnp.einsum('sxcf,xfd->sxcd', hidden_e, expert_down, preferred_element_typ...  14.8 us
    reduce_sum x1, other arithmetic, per_device(): expert_sum = jnp.sum(picked * route_weight[:, :, None], axis=1)  12.9 us
  transfers between devices with their start and end apart: 3, of which 2 were waited for; matrix products, arithmetic and copies ran while one was open for 1% of the time, Pallas kernels for 0%

commit v1 on v0

v1 whole, which is shorter than its diff:
```python
import jax
import jax.numpy as jnp
from jax import lax
from jax.experimental import pallas as pl
from jax.experimental.pallas import tpu as pltpu
from jax.sharding import PartitionSpec as P

F32, BF16 = jnp.float32, jnp.bfloat16
WIDTHS = (1280, 1152, 1152)
STARTS = (0, 1280, 2432)
HALF = 3584
GATHER = ((1, 2, 0), (2, 0, 1), (0, 1, 2))
REDUCE = ((0, 1, 2), (1, 2, 0), (2, 0, 1))
STEPS = (1, 3, 2)
LINES = (0, 3, 1, 2)
PLANES = (0, 3, 1, 2)
ALL = slice(None)


def position():
    e, t = lax.axis_index("expert"), lax.axis_index("tensor")
    x = lax.div(t, 8) * 2 + lax.div(e, 4)
    y = lax.rem(lax.div(t, 2), 4)
    z = lax.rem(e, 4)
    return (x, y, z), lax.rem(t, 2)


def device(pos, core):
    x, y, z = pos
    return (lax.rem(x, 2) * 4 + z, (lax.div(x, 2) * 4 + y) * 2 + core)


def moved(pos, axis, step):
    return tuple(lax.rem(p + step, 4) if a == axis else p for a, p in enumerate(pos))


def at(parts):
    return tuple(parts[a] for a in range(3))


def greet(pos, core):
    barrier = pltpu.get_barrier_semaphore()
    others = [device(moved(pos, a, s), core) for a in range(3) for s in STEPS]
    others.append(device(pos, 1 - core))
    for other in others:
        pl.semaphore_signal(barrier, inc=1, device_id=other, device_id_type=pl.DeviceIdType.MESH)
    pl.semaphore_wait(barrier, len(others))


def remote(src, dst, send, recv, target):
    return pltpu.make_async_remote_copy(
        src_ref=src,
        dst_ref=dst,
        send_sem=send,
        recv_sem=recv,
        device_id=target,
        device_id_type=pl.DeviceIdType.MESH,
    )


def dot(a, b):
    return jnp.dot(a, b, preferred_element_type=F32)


def dot_t(a, b):
    return lax.dot_general(a, b, (((1,), (1,)), ((), ())), preferred_element_type=F32)


def block_kernel(
    tok, ids, gains, gain, wg_e, wu_e, wg_d, wu_d, wd_e, wd_d,
    out,
    x0, x1, x2, mine, other,
    down_e, down_d, he, he_in, heb, hd, hd_in, hdb, weight,
    a0, a1, a2, b0, b1, b2, c0, c1, c2, d0, d1, d2, t0, t1, t2, fin_s, fin_r,
    w_sem, down_s, down_r, pair_s, pair_r, g1s, g1r, g2s, g2r, g3s, g3r, fs, fr,
    he_s, he_r, hd_s, hd_r, s1, r1, s2, r2, s3, r3, f_s, f_r,
):
    xs = (x0, x1, x2)
    pos, core = position()
    rest = 1 - core
    sibling = device(pos, rest)
    own_cols = pl.ds(pl.multiple_of(core * HALF, 128), HALF)
    rest_cols = pl.ds(pl.multiple_of(rest * HALF, 128), HALF)
    x_low = lax.rem(pos[0], 2)
    first = core == 0
    lower, upper = slice(0, 2), slice(2, 4)
    sends = []

    def go(copy):
        copy.start()
        sends.append(copy)

    def settle():
        for copy in sends:
            copy.wait_send()
        sends.clear()

    def gather(up_e, up_d, acc, acc_d):
        top, low = pl.ds(0, 304), pl.ds(304, 304)
        loads = [
            pltpu.make_async_copy(src, dst, w_sem.at[i])
            for i, (src, dst) in enumerate((
                (wg_e, up_e.at[top]), (wu_e, up_e.at[low]), (wg_d, up_d.at[top]), (wu_d, up_d.at[low]),
                (wd_e.at[:, own_cols], down_e.at[top]), (wd_d.at[:, own_cols], down_d.at[top]),
            ))
        ]
        for load in loads:
            load.start()
        floats = tok[...].astype(F32)
        normed = floats * lax.rsqrt(jnp.mean(floats * floats, axis=1, keepdims=True) + 1e-05) * gain[...]
        lane = lax.broadcasted_iota(jnp.int32, (8, 128), 1).astype(F32)
        same = lax.broadcasted_iota(jnp.int32, (8, 8), 0) == lax.broadcasted_iota(jnp.int32, (8, 8), 1)
        extra = jnp.zeros((8, 128), F32)
        for k in range(2):
            g, who = (
                jnp.sum(jnp.where(same, ref[k : k + 1, :].astype(F32), 0.0), axis=1, keepdims=True)
                for ref in (gains, ids)
            )
            high = jnp.floor(g * (1.0 / 32.0))
            extra = extra + jnp.where(lane == who, high, 0.0)
            extra = extra + jnp.where(lane == who + 8.0, g - high * 32.0, 0.0)
        for h in range(2):
            mine[h, :, :HALF] = normed[:, h * HALF : (h + 1) * HALF].astype(BF16)
            mine[h, :, HALF:] = extra.astype(BF16)
        greet(pos, core)
        swap = remote(mine.at[rest], other, pair_s, pair_r, sibling)
        go(swap)
        lends = [
            remote(src.at[:, rest_cols], dst.at[low], down_s.at[i], down_r.at[i], sibling)
            for i, (src, dst) in enumerate(((wd_e, down_e), (wd_d, down_d)))
        ]
        swap.wait_recv()
        a, b = mine[core].astype(F32), other[...].astype(F32)
        slab = jnp.concatenate([jnp.where(first, a, b), jnp.where(first, b, a)], axis=0).astype(BF16)
        for j in range(3):
            wide = xs[j].shape[-1]
            xs[j][(core, *pos)] = slab[:, STARTS[j] : STARTS[j] + wide]

        def copy(j, idx, sem_s, sem_r, target, half=None):
            ref = xs[j].at[(core if half is None else half, *idx)]
            return remote(ref, ref, sem_s, sem_r, target)

        for j in range(3):
            axis = GATHER[j][0]
            for k, d in enumerate(STEPS):
                go(copy(j, pos, g1s.at[j, k], g1r.at[j, k], device(moved(pos, axis, d), core)))
        for lend in lends:
            go(lend)
        acc[...] = jnp.zeros_like(acc)
        acc_d[...] = jnp.zeros_like(acc_d)

        sides = ((3, lower, 1), (1, upper, 3))

        def line(j, n, m, part=ALL):
            a1, a2, a3 = GATHER[j]
            return at({a1: part, a2: lax.rem(pos[a2] + LINES[n], 4), a3: lax.rem(pos[a3] + PLANES[m], 4)})

        def plane(j, m):
            a1, a2, a3 = GATHER[j]
            return at({a1: ALL, a2: ALL, a3: lax.rem(pos[a3] + PLANES[m], 4)})

        def forward(j, n, m):
            go(copy(j, line(j, n, m), fs.at[j, n, m], fr.at[j, n, m], sibling))

        def forwarded(m):
            for j in range(3):
                for n in range(4):
                    copy(j, line(j, n, m), fs.at[j, n, m], fr.at[j, n, m], sibling, rest).wait_recv()

        def own(j, n):
            axis = GATHER[j][2]
            for k, d in enumerate((1, 3)):
                go(copy(j, line(j, n, 0), g3s.at[j, n, k], g3r.at[j, n, k], device(moved(pos, axis, d), core)))
            forward(j, n, 0)

        def relay(j, n):
            axis = GATHER[j][2]
            for k, (came, part, d) in enumerate(sides):
                m = 1 + k
                copy(j, line(j, n, m), g3s.at[j, n, k], g3r.at[j, n, k], sibling).wait_recv()
                target = device(moved(pos, axis, d), core)
                go(copy(j, line(j, n, m, part), g3s.at[j, n, 2 + k], g3r.at[j, n, 2 + k], target))
                forward(j, n, m)

        def add(j, idx, half):
            rows = xs[j][(half, *idx)].reshape(256, xs[j].shape[-1])[:, : WIDTHS[j]]
            span = pl.ds(pl.multiple_of(half * HALF + STARTS[j], 128), WIDTHS[j])
            acc[idx] += dot_t(rows, up_e[:, span]).reshape(4, 4, 16, 608)

        def add_dense(j):
            for h in range(2):
                rows = jnp.concatenate(
                    [
                        xs[j][h, x_low + 2 * k, :, pos[2]].reshape(64, xs[j].shape[-1])[:, : WIDTHS[j]]
                        for k in range(2)
                    ],
                    axis=0,
                )
                acc_d[...] += dot_t(rows, up_d[:, h * HALF + STARTS[j] : h * HALF + STARTS[j] + WIDTHS[j]])

        def adds(m, half):
            for j in range(3):
                add(j, plane(j, m), half)

        for j in range(3):
            axis = GATHER[j][0]
            for k, d in enumerate(STEPS):
                copy(j, moved(pos, axis, 4 - d), g1s.at[j, k], g1r.at[j, k], sibling).wait_recv()
            axis = GATHER[j][1]
            for k, d in enumerate((1, 3)):
                go(copy(j, line(j, 0, 0), g2s.at[j, k], g2r.at[j, k], device(moved(pos, axis, d), core)))
            own(j, 0)
        for j in range(3):
            axis = GATHER[j][1]
            for k, (came, part, d) in enumerate(sides):
                n = 1 + k
                copy(j, line(j, n, 0), g2s.at[j, k], g2r.at[j, k], sibling).wait_recv()
                target = device(moved(pos, axis, d), core)
                go(copy(j, line(j, n, 0, part), g2s.at[j, 2 + k], g2r.at[j, 2 + k], target))
                own(j, n)
        for j in range(3):
            relay(j, 0)
        for j in range(3):
            for k, part in enumerate((lower, upper)):
                copy(j, line(j, 3, 0, part), g2s.at[j, 2 + k], g2r.at[j, 2 + k], sibling).wait_recv()
            own(j, 3)
        for load in loads:
            load.wait()
        for j in range(3):
            relay(j, 1)
            add(j, plane(j, 0), core)
        for j in range(3):
            relay(j, 2)
        forwarded(0)
        adds(0, rest)
        add_dense(2)
        for j in range(3):
            relay(j, 3)
        adds(1, core)
        adds(2, core)

        def last(n):
            for j in range(3):
                for k, part in enumerate((lower, upper)):
                    copy(j, line(j, n, 3, part), g3s.at[j, n, 2 + k], g3r.at[j, n, 2 + k], sibling).wait_recv()
                forward(j, n, 3)

        last(0)
        last(1)
        forwarded(1)
        adds(1, rest)
        last(2)
        forwarded(2)
        adds(2, rest)
        last(3)
        adds(3, core)
        forwarded(3)
        adds(3, rest)

        def glu(v):
            g, u = v[:, :304], v[:, 304:]
            return (g / (1.0 + jnp.exp(-g)) * u).astype(BF16)

        e = lax.axis_index("expert")
        lanes = lax.broadcasted_iota(jnp.int32, (256, 128), 1)
        pick = jnp.where(lanes == e, 32.0, 0.0) + jnp.where(lanes == e + 8, 1.0, 0.0)
        trades = [remote(he.at[x], he_in.at[x], he_s.at[x], he_r.at[x], sibling) for x in range(4)]
        for x in range(4):
            he[x] = glu(acc[x].reshape(256, 608)).reshape(4, 4, 16, 304)
            go(trades[x])
        for x in range(4):
            pieces = x2[core, x, :, :, :, WIDTHS[2] :].reshape(256, 128).astype(F32)
            weight[x] = (jnp.sum(pieces * pick, axis=1, keepdims=True) * (1.0 / 1024.0)).reshape(4, 4, 16, 1)
        add_dense(0)
        add_dense(1)
        hd[...] = glu(acc_d[...])
        go(remote(hd, hd_in, hd_s, hd_r, sibling))
        for x in range(4):
            trades[x].wait_recv()
            heb[x] = jnp.concatenate([he[x].reshape(256, 304), he_in[x].reshape(256, 304)], axis=1).reshape(4, 4, 16, 608)
        for lend in lends:
            lend.wait_recv()
        settle()

    def reduce(z0, z1, z2, q0, q1, q2):
        zs, dense = (z0, z1, z2), (q0, q1, q2)
        half1, full1, half2, full2, last_in = (a0, a1, a2), (b0, b1, b2), (c0, c1, c2), (d0, d1, d2), (t0, t1, t2)

        def where(j, step):
            b1, b2, b3 = REDUCE[j]
            return at({b1: lax.rem(pos[b1] + step, 4), b2: ALL, b3: ALL})

        def produce(j, step):
            cols = slice(STARTS[j], STARTS[j] + WIDTHS[j])
            idx = where(j, step)
            part = dot(heb[idx].reshape(256, 608), down_e[:, cols]) * weight[idx].reshape(256, 1)
            zs[j][idx] = part.astype(BF16).reshape(4, 4, 16, WIDTHS[j])

        def produce_dense(j, step):
            idx = where(j, step)
            axis = REDUCE[j][0]
            places = []
            if axis == 0 and step % 2 == 0:
                places = [((idx[0], ALL, pos[2]), (lax.div(idx[0], 2), ALL))]
            elif axis == 1:
                places = [((x_low + 2 * k, idx[1], pos[2]), (k, idx[1])) for k in range(2)]
            elif axis == 2 and step == 0:
                places = [((x_low + 2 * k, ALL, pos[2]), (k, ALL)) for k in range(2)]
            for spot, src in places:
                zs[j][spot] = (zs[j][spot].astype(F32) + dense[j][src]).astype(BF16)

        def gain(j, idx, *others):
            total = zs[j][idx].astype(F32)
            for other in others:
                total = total + other[...].astype(F32)
            zs[j][idx] = total.astype(BF16)

        def row(j, step, r, part=ALL):
            b1, b2, b3 = REDUCE[j]
            return at({b1: lax.rem(pos[b1] + step, 4), b2: lax.rem(pos[b2] + r, 4), b3: part})

        def halves(j, step, r, axis, bufs, ss, rr):
            for k, (part, d) in enumerate(((lower, 1), (upper, 3))):
                go(remote(zs[j].at[row(j, step, r, part)], bufs.at[k], ss.at[k], rr.at[k], device(moved(pos, axis, d), core)))

        def whole(j, step, r, axis, k, bufs, fulls, ss, rr):
            part, d = ((lower, 1), (upper, 3))[k]
            remote(bufs.at[k], bufs.at[k], ss.at[k], rr.at[k], sibling).wait_recv()
            gain(j, row(j, step, r, part), bufs.at[k])
            go(remote(zs[j].at[row(j, step, r)], fulls.at[k], ss.at[2 + k], rr.at[2 + k], device(moved(pos, axis, d), core)))

        def close(j, r, fulls, ss, rr):
            for k in range(2):
                remote(fulls.at[k], fulls.at[k], ss.at[2 + k], rr.at[2 + k], sibling).wait_recv()
            gain(j, row(j, 0, r), fulls.at[0], fulls.at[1])

        def outer(j, n):
            return (half1[j].at[n], full1[j].at[n], s1.at[j, n], r1.at[j, n])

        def inner(j):
            return (half2[j], full2[j], s2.at[j], r2.at[j])

        order = (2, 1, 3, 0)
        for n, step in enumerate(order):
            for j in range(3):
                produce(j, step)
            if n == 0:
                remote(hd, hd_in, hd_s, hd_r, sibling).wait_recv()
                hdb[...] = jnp.concatenate([hd[...], hd_in[...]], axis=1)
                for j in range(3):
                    part = dot(hdb[...], down_d[:, STARTS[j] : STARTS[j] + WIDTHS[j]])
                    dense[j][...] = part.reshape(2, 4, 16, WIDTHS[j])
            for j in range(3):
                produce_dense(j, step)
                for i, r in enumerate(order):
                    bufs, fulls, ss, rr = outer(j, i)
                    if step == 2:
                        halves(j, 2, r, REDUCE[j][0], bufs, ss, rr)
                    elif step:
                        whole(j, step, r, REDUCE[j][0], n - 1, bufs, fulls, ss, rr)
        for i, r in enumerate(order):
            for j in range(3):
                _, fulls, ss, rr = outer(j, i)
                close(j, r, fulls, ss, rr)
                bufs, fulls, ss, rr = inner(j)
                if r == 2:
                    halves(j, 0, r, REDUCE[j][1], bufs, ss, rr)
                elif r:
                    whole(j, 0, r, REDUCE[j][1], i - 1, bufs, fulls, ss, rr)
        for j in range(3):
            _, fulls, ss, rr = inner(j)
            close(j, 0, fulls, ss, rr)
            axis = REDUCE[j][2]
            for k, d in enumerate(STEPS):
                there = moved(pos, axis, d)
                go(remote(zs[j].at[there], last_in[j].at[k], s3.at[j, k], r3.at[j, k], device(there, core)))
        keep = []
        for j in range(3):
            total = zs[j][pos].astype(F32)
            for k in range(3):
                remote(last_in[j].at[k], last_in[j].at[k], s3.at[j, k], r3.at[j, k], sibling).wait_recv()
                total = total + last_in[j][k].astype(F32)
            keep.append(jnp.where(first, total[:8], total[8:]))
            fin_s[:, STARTS[j] : STARTS[j] + WIDTHS[j]] = jnp.where(first, total[8:], total[:8])
        swap = remote(fin_s, fin_r, f_s, f_r, sibling)
        go(swap)
        for j in range(3):
            cols = pl.ds(pl.multiple_of(core * HALF + STARTS[j], 128), WIDTHS[j])
            out[:, cols] = (tok[:, cols].astype(F32) + keep[j]).astype(BF16)
        swap.wait_recv()
        out[:, rest_cols] = (tok[:, rest_cols].astype(F32) + fin_r[...]).astype(BF16)
        settle()

    wide = (608, tok.shape[1])
    pl.run_scoped(
        gather,
        pltpu.VMEM(wide, BF16),
        pltpu.VMEM(wide, BF16),
        pltpu.VMEM((4, 4, 4, 16, 608), F32),
        pltpu.VMEM((128, 608), F32),
    )
    pl.run_scoped(
        reduce,
        *(pltpu.VMEM((4, 4, 4, 16, w), BF16) for w in WIDTHS),
        *(pltpu.VMEM((2, 4, 16, w), F32) for w in WIDTHS),
    )


def per_device(
    tokens, route_ids, route_gain, norm_gain, dense_gate, dense_up, dense_down, expert_gate, expert_up, expert_down
):
    vmem = pl.BlockSpec(memory_space=pltpu.VMEM)
    hbm = pl.BlockSpec(memory_space=pl.ANY)
    dma = pltpu.SemaphoreType.DMA
    d, f = dense_gate.shape

    def sized(*lead):
        return [pltpu.VMEM((*lead, w), BF16) for w in WIDTHS]

    gathered = [pltpu.VMEM((2, 4, 4, 4, 16, w + (128 if j == 2 else 0)), BF16) for j, w in enumerate(WIDTHS)]
    return pl.pallas_call(
        block_kernel,
        out_shape=jax.ShapeDtypeStruct(tokens.shape, BF16),
        in_specs=[vmem] * 4 + [hbm] * 6,
        out_specs=vmem,
        scratch_shapes=gathered
        + [pltpu.VMEM((2, 8, HALF + 128), BF16), pltpu.VMEM((8, HALF + 128), BF16)]
        + [pltpu.VMEM((2 * f, HALF), BF16)] * 2
        + [pltpu.VMEM((4, 4, 4, 16, f), BF16)] * 2
        + [pltpu.VMEM((4, 4, 4, 16, 2 * f), BF16)]
        + [pltpu.VMEM((128, f), BF16)] * 2
        + [pltpu.VMEM((128, 2 * f), BF16), pltpu.VMEM((4, 4, 4, 16, 1), F32)]
        + sized(4, 2, 2, 16)
        + sized(4, 2, 4, 16)
        + sized(2, 2, 16)
        + sized(2, 4, 16)
        + sized(3, 16)
        + [pltpu.VMEM((8, HALF), F32)] * 2
        + [dma((6,)), dma((2,)), dma((2,)), dma, dma]
        + [dma((3, 3))] * 2
        + [dma((3, 4))] * 2
        + [dma((3, 4, 4))] * 4
        + [dma((4,)), dma((4,)), dma, dma]
        + [dma((3, 4, 4))] * 2
        + [dma((3, 4))] * 2
        + [dma((3, 3))] * 2
        + [dma, dma],
        compiler_params=pltpu.CompilerParams(
            collective_id=0, has_side_effects=True, vmem_limit_bytes=60 * 1024 * 1024
        ),
        name="gather_experts_sum",
    )(
        tokens, route_ids.T, route_gain.T, norm_gain.reshape(1, d),
        expert_gate.reshape(d, f).T, expert_up.reshape(d, f).T, dense_gate.T, dense_up.T,
        expert_down.reshape(f, d), dense_down,
    )


def solution(mesh):
    rows = P(("expert", "tensor"), None)
    return jax.shard_map(
        per_device,
        mesh=mesh,
        in_specs=(
            rows, rows, rows, P(),
            P(None, "tensor"), P(None, "tensor"), P("tensor", None),
            P("expert", None, "tensor"), P("expert", None, "tensor"), P("expert", "tensor", None),
        ),
        out_specs=rows,
        check_vma=False,
    )
```

time: 503 us -> 102 us (0.20)
  blocking collectives: 209 us -> 0 us
  local copies, waits for them, and re-layouts: 128 us -> 1.55 us
  Pallas kernels: 0 us -> 100 us
  waiting for transfers between devices: 91.5 us -> 0 us
  matrix products: 34.7 us -> 0 us
  other arithmetic: 19.2 us -> 0 us
  between operations: 13.5 us -> 0.01 us
    all_gather x2 -> x0, blocking collectives: 123 us -> none  [the longest x1 96.7 us: per_device(): lax.all_gather(route_gain, 'tensor', axis=0, tiled=True)]
    pallas_call x0 -> x1, Pallas kernels: none -> 100 us  [per_device(): pl.pallas_call(block_kernel, out_shape=jax.ShapeDtypeStruct(tokens.shape,...]
    scatter x1 -> x0, local copies, waits for them, and re-layouts: 95.6 us -> none  [per_device(): outgoing = jnp.zeros((experts, capacity, row_width), jnp.bfloat16).at[fla...]
    all_to_all x1 -> x0, blocking collectives: 86.7 us -> none  [per_device(): lax.all_to_all(outgoing, 'expert', split_axis=0, concat_axis=0, tiled=True)]
    reduce_scatter x1 -> x0, waiting for transfers between devices: 65.4 us -> none  [per_device(): lax.psum_scatter((dense_part + expert_sum).astype(jnp.bfloat16), 'tensor'...]
    dot_general x4 -> x0, matrix products: 34.7 us -> none  [the longest x1 14.8 us: per_device(): jnp.einsum('sxcf,xfd->sxcd', hidden_e, expert_down, preferred_element_typ...]
    all_gather x1 -> x0, waiting for transfers between devices: 25.3 us -> none  [per_device(): lax.all_gather(tokens, 'tensor', axis=0, tiled=True)]
    gather x2 -> x0, local copies, waits for them, and re-layouts: 15.9 us -> none  [the longest x1 11.2 us: per_device(): back[flat_ids, slot_rank].astype(jnp.float32)]
  transfers between devices with their start and end apart: 3 -> 0, of which waited for: 2 -> 0; matrix products, arithmetic and copies ran while one was open for 1% -> 0% of each run, Pallas kernels for 0% -> 0%
where the time goes in v1:
time: 102 us
  Pallas kernels  100 us (98%)
  local copies, waits for them, and re-layouts  1.55 us (2%)
    pallas_call x1, Pallas kernels, per_device(): pl.pallas_call(block_kernel, out_shape=jax.ShapeDtypeStruct(tokens.shape,...  100 us

profile of v1, /device:TPU:1, one launch (start us, length us, event | category | flops | bytes accessed | tf_op | source)
XLA Modules:
  0.0 101.7 jit_solution(5850320343426901619)
XLA Ops:
  0.0 100.2 %gather_experts_sum.1 = bf16[8,7168]{1,0:T(8,128)(2,1)} custom-call(bf16[8,7168]{1,0:T(8,128)(2,1)} %tok.1, s32[2,8]{1,0:T(2,128)} %bitcast.18, s32[2,8]{1,0:T(2,128)} %bitcast.19, f32[1,7168]{1,0:T(1,128)} %bitcast.17, bf16[304,7168]{1,0:T(8,128)(2,1)} %bitcast.12, bf16[304,7168]{1,0:T(8,128)(2,1)} %bitcast.13, bf16[304,7168]{1,0:T(8,128)(2,1)} %bitcast.14, ...), custom_call_target="tpu_custom_call" | custom-call | tf_op jit(solution)/shard_map/gather_experts_sum/pallas_call | solution.py:421
  100.2 1.6 %copy.12 = bf16[8,7168]{1,0:T(8,128)(2,1)} copy(bf16[8,7168]{1,0:T(8,128)(2,1)} %gather_experts_sum.1) | data formatting | bytes 229376

commit v2 on v1

--- a/solution.py
+++ b/solution.py
@@ -40,11 +40,11 @@
 
 def greet(pos, core):
     barrier = pltpu.get_barrier_semaphore()
-    others = [device(moved(pos, a, s), core) for a in range(3) for s in STEPS]
+    others = [device(moved(pos, a, s), c) for a in range(3) for s in STEPS for c in (core, 1 - core)]
     others.append(device(pos, 1 - core))
     for other in others:
         pl.semaphore_signal(barrier, inc=1, device_id=other, device_id_type=pl.DeviceIdType.MESH)
-    pl.semaphore_wait(barrier, len(others))
+    return lambda: pl.semaphore_wait(barrier, len(others))
 
 
 def remote(src, dst, send, recv, target):
@@ -69,11 +69,11 @@
 def block_kernel(
     tok, ids, gains, gain, wg_e, wu_e, wg_d, wu_d, wd_e, wd_d,
     out,
-    x0, x1, x2, mine, other,
+    x0, x1, x2, mine, other, n0, n1, n2,
     down_e, down_d, he, he_in, heb, hd, hd_in, hdb, weight,
-    a0, a1, a2, b0, b1, b2, c0, c1, c2, d0, d1, d2, t0, t1, t2, fin_s, fin_r,
+    a0, a1, a2, b0, b1, b2, c0, c1, c2, d0, d1, d2, t0, t1, t2, u0, u1, u2,
     w_sem, down_s, down_r, pair_s, pair_r, g1s, g1r, g2s, g2r, g3s, g3r, fs, fr,
-    he_s, he_r, hd_s, hd_r, s1, r1, s2, r2, s3, r3, f_s, f_r,
+    he_s, he_r, hd_s, hd_r, s1, r1, s2, r2, s3, r3,
 ):
     xs = (x0, x1, x2)
     pos, core = position()
@@ -104,6 +104,7 @@
                 (wd_e.at[:, own_cols], down_e.at[top]), (wd_d.at[:, own_cols], down_d.at[top]),
             ))
         ]
+        met = greet(pos, core)
         for load in loads:
             load.start()
         floats = tok[...].astype(F32)
@@ -122,28 +123,26 @@
         for h in range(2):
             mine[h, :, :HALF] = normed[:, h * HALF : (h + 1) * HALF].astype(BF16)
             mine[h, :, HALF:] = extra.astype(BF16)
-        greet(pos, core)
+        met()
+        near = (n0, n1, n2)
+        for j in range(3):
+            span = slice(STARTS[j], STARTS[j] + xs[j].shape[-1])
+            for k, d in enumerate(STEPS):
+                there = moved(pos, GATHER[j][0], d)
+                for i, half in enumerate((core, rest)):
+                    target = device(there, half)
+                    src = mine.at[half, :, span]
+                    go(remote(src, near[j].at[k, core], g1s.at[j, k, i], g1r.at[j, k, core], target))
         swap = remote(mine.at[rest], other, pair_s, pair_r, sibling)
         go(swap)
         lends = [
             remote(src.at[:, rest_cols], dst.at[low], down_s.at[i], down_r.at[i], sibling)
             for i, (src, dst) in enumerate(((wd_e, down_e), (wd_d, down_d)))
         ]
-        swap.wait_recv()
-        a, b = mine[core].astype(F32), other[...].astype(F32)
-        slab = jnp.concatenate([jnp.where(first, a, b), jnp.where(first, b, a)], axis=0).astype(BF16)
-        for j in range(3):
-            wide = xs[j].shape[-1]
-            xs[j][(core, *pos)] = slab[:, STARTS[j] : STARTS[j] + wide]
-
         def copy(j, idx, sem_s, sem_r, target, half=None):
             ref = xs[j].at[(core if half is None else half, *idx)]
             return remote(ref, ref, sem_s, sem_r, target)
 
-        for j in range(3):
-            axis = GATHER[j][0]
-            for k, d in enumerate(STEPS):
-                go(copy(j, pos, g1s.at[j, k], g1r.at[j, k], device(moved(pos, axis, d), core)))
         for lend in lends:
             go(lend)
         acc[...] = jnp.zeros_like(acc)
@@ -162,9 +161,9 @@
         def forward(j, n, m):
             go(copy(j, line(j, n, m), fs.at[j, n, m], fr.at[j, n, m], sibling))
 
-        def forwarded(m):
+        def forwarded(m, lines=range(4)):
             for j in range(3):
-                for n in range(4):
+                for n in lines:
                     copy(j, line(j, n, m), fs.at[j, n, m], fr.at[j, n, m], sibling, rest).wait_recv()
 
         def own(j, n):
@@ -198,14 +197,33 @@
                 )
                 acc_d[...] += dot_t(rows, up_d[:, h * HALF + STARTS[j] : h * HALF + STARTS[j] + WIDTHS[j]])
 
+        def add_lines(m, half, lines):
+            for j in range(3):
+                rows = jnp.concatenate(
+                    [xs[j][(half, *line(j, n, m))].reshape(64, xs[j].shape[-1])[:, : WIDTHS[j]] for n in lines], axis=0
+                )
+                span = pl.ds(pl.multiple_of(half * HALF + STARTS[j], 128), WIDTHS[j])
+                part = dot_t(rows, up_e[:, span])
+                for i, n in enumerate(lines):
+                    acc[line(j, n, m)] += part[i * 64 : i * 64 + 64].reshape(4, 16, 608)
+
         def adds(m, half):
             for j in range(3):
                 add(j, plane(j, m), half)
 
-        for j in range(3):
-            axis = GATHER[j][0]
+        def stack(a, b):
+            return jnp.concatenate([a.astype(F32), b.astype(F32)], axis=0).astype(BF16)
+
+        swap.wait_recv()
+        a, b = mine[core].astype(F32), other[...].astype(F32)
+        slab = stack(jnp.where(first, a, b), jnp.where(first, b, a))
+        for j in range(3):
+            xs[j][(core, *pos)] = slab[:, STARTS[j] : STARTS[j] + xs[j].shape[-1]]
             for k, d in enumerate(STEPS):
-                copy(j, moved(pos, axis, 4 - d), g1s.at[j, k], g1r.at[j, k], sibling).wait_recv()
+                for c in range(2):
+                    got = near[j].at[k, c]
+                    remote(got, got, g1s.at[j, k, c], g1r.at[j, k, c], sibling).wait_recv()
+                xs[j][(core, *moved(pos, GATHER[j][0], 4 - d))] = stack(near[j][k, 0], near[j][k, 1])
             axis = GATHER[j][1]
             for k, d in enumerate((1, 3)):
                 go(copy(j, line(j, 0, 0), g2s.at[j, k], g2r.at[j, k], device(moved(pos, axis, d), core)))
@@ -252,10 +270,14 @@
         last(2)
         forwarded(2)
         adds(2, rest)
+        add_lines(3, core, (0, 1))
+        forwarded(3, (0, 1))
+        add_lines(3, rest, (0, 1))
+        add_dense(0)
         last(3)
-        adds(3, core)
-        forwarded(3)
-        adds(3, rest)
+        add_lines(3, core, (2, 3))
+        forwarded(3, (2, 3))
+        add_lines(3, rest, (2, 3))
 
         def glu(v):
             g, u = v[:, :304], v[:, 304:]
@@ -271,7 +293,6 @@
         for x in range(4):
             pieces = x2[core, x, :, :, :, WIDTHS[2] :].reshape(256, 128).astype(F32)
             weight[x] = (jnp.sum(pieces * pick, axis=1, keepdims=True) * (1.0 / 1024.0)).reshape(4, 4, 16, 1)
-        add_dense(0)
         add_dense(1)
         hd[...] = glu(acc_d[...])
         go(remote(hd, hd_in, hd_s, hd_r, sibling))
@@ -285,6 +306,7 @@
     def reduce(z0, z1, z2, q0, q1, q2):
         zs, dense = (z0, z1, z2), (q0, q1, q2)
         half1, full1, half2, full2, last_in = (a0, a1, a2), (b0, b1, b2), (c0, c1, c2), (d0, d1, d2), (t0, t1, t2)
+        staged = (u0, u1, u2)
 
         def where(j, step):
             b1, b2, b3 = REDUCE[j]
@@ -341,24 +363,41 @@
             return (half2[j], full2[j], s2.at[j], r2.at[j])
 
         order = (2, 1, 3, 0)
-        for n, step in enumerate(order):
+        def begin(j):
+            for i, r in enumerate(order):
+                bufs, _, ss, rr = outer(j, i)
+                halves(j, 2, r, REDUCE[j][0], bufs, ss, rr)
+
+        def go_on(j, i, k):
+            bufs, fulls, ss, rr = outer(j, i)
+            whole(j, order[1 + k], order[i], REDUCE[j][0], k, bufs, fulls, ss, rr)
+
+        produce(2, 2)
+        begin(2)
+        remote(hd, hd_in, hd_s, hd_r, sibling).wait_recv()
+        hdb[...] = jnp.concatenate([hd[...], hd_in[...]], axis=1)
+        for j in range(3):
+            part = dot(hdb[...], down_d[:, STARTS[j] : STARTS[j] + WIDTHS[j]])
+            dense[j][...] = part.reshape(2, 4, 16, WIDTHS[j])
+            if j < 2:
+                produce(j, 2)
+                produce_dense(j, 2)
+                begin(j)
+        for k in range(2):
             for j in range(3):
-                produce(j, step)
-            if n == 0:
-                remote(hd, hd_in, hd_s, hd_r, sibling).wait_recv()
-                hdb[...] = jnp.concatenate([hd[...], hd_in[...]], axis=1)
+                produce(j, order[1 + k])
+                produce_dense(j, order[1 + k])
+            for i in range(3):
                 for j in range(3):
-                    part = dot(hdb[...], down_d[:, STARTS[j] : STARTS[j] + WIDTHS[j]])
-                    dense[j][...] = part.reshape(2, 4, 16, WIDTHS[j])
-            for j in range(3):
-                produce_dense(j, step)
-                for i, r in enumerate(order):
-                    bufs, fulls, ss, rr = outer(j, i)
-                    if step == 2:
-                        halves(j, 2, r, REDUCE[j][0], bufs, ss, rr)
-                    elif step:
-                        whole(j, step, r, REDUCE[j][0], n - 1, bufs, fulls, ss, rr)
+                    go_on(j, i, k)
+        for j in range(3):
+            produce(j, 0)
+            produce_dense(j, 0)
         for i, r in enumerate(order):
+            if i == 2:
+                for j in range(3):
+                    for k in range(2):
+                        go_on(j, 3, k)
             for j in range(3):
                 _, fulls, ss, rr = outer(j, i)
                 close(j, r, fulls, ss, rr)
@@ -370,25 +409,24 @@
         for j in range(3):
             _, fulls, ss, rr = inner(j)
             close(j, 0, fulls, ss, rr)
-            axis = REDUCE[j][2]
-            for k, d in enumerate(STEPS):
-                there = moved(pos, axis, d)
-                go(remote(zs[j].at[there], last_in[j].at[k], s3.at[j, k], r3.at[j, k], device(there, core)))
-        keep = []
-        for j in range(3):
-            total = zs[j][pos].astype(F32)
-            for k in range(3):
-                remote(last_in[j].at[k], last_in[j].at[k], s3.at[j, k], r3.at[j, k], sibling).wait_recv()
-                total = total + last_in[j][k].astype(F32)
-            keep.append(jnp.where(first, total[:8], total[8:]))
-            fin_s[:, STARTS[j] : STARTS[j] + WIDTHS[j]] = jnp.where(first, total[8:], total[:8])
-        swap = remote(fin_s, fin_r, f_s, f_r, sibling)
-        go(swap)
-        for j in range(3):
-            cols = pl.ds(pl.multiple_of(core * HALF + STARTS[j], 128), WIDTHS[j])
-            out[:, cols] = (tok[:, cols].astype(F32) + keep[j]).astype(BF16)
-        swap.wait_recv()
-        out[:, rest_cols] = (tok[:, rest_cols].astype(F32) + fin_r[...]).astype(BF16)
+            for k, d in enumerate((*STEPS, 0)):
+                there = moved(pos, REDUCE[j][2], d)
+                rows = zs[j][there].astype(F32)
+                for c in range(2):
+                    staged[j][k, c] = rows[c * 8 : c * 8 + 8].astype(BF16)
+                for i, c in enumerate((core, rest)):
+                    if d or i:
+                        src, dst = staged[j].at[k, c], last_in[j].at[k, core]
+                        go(remote(src, dst, s3.at[j, k, i], r3.at[j, k, core], device(there, c)))
+        for j in range(3):
+            for i, half in enumerate((core, rest)):
+                total = staged[j][3, core].astype(F32) if i == 0 else 0.0
+                for k in range(3 + i):
+                    got = last_in[j].at[k, half]
+                    remote(got, got, s3.at[j, k, i], r3.at[j, k, half], sibling).wait_recv()
+                    total = total + got[...].astype(F32)
+                cols = pl.ds(pl.multiple_of(half * HALF + STARTS[j], 128), WIDTHS[j])
+                out[:, cols] = (tok[:, cols].astype(F32) + total).astype(BF16)
         settle()
 
     wide = (608, tok.shape[1])
@@ -425,6 +463,7 @@
         out_specs=vmem,
         scratch_shapes=gathered
         + [pltpu.VMEM((2, 8, HALF + 128), BF16), pltpu.VMEM((8, HALF + 128), BF16)]
+        + [pltpu.VMEM((3, 2, 8, x.shape[-1]), BF16) for x in gathered]
         + [pltpu.VMEM((2 * f, HALF), BF16)] * 2
         + [pltpu.VMEM((4, 4, 4, 16, f), BF16)] * 2
         + [pltpu.VMEM((4, 4, 4, 16, 2 * f), BF16)]
@@ -434,17 +473,16 @@
         + sized(4, 2, 4, 16)
         + sized(2, 2, 16)
         + sized(2, 4, 16)
-        + sized(3, 16)
-        + [pltpu.VMEM((8, HALF), F32)] * 2
+        + sized(4, 2, 8)
+        + sized(4, 2, 8)
         + [dma((6,)), dma((2,)), dma((2,)), dma, dma]
-        + [dma((3, 3))] * 2
+        + [dma((3, 3, 2))] * 2
         + [dma((3, 4))] * 2
         + [dma((3, 4, 4))] * 4
         + [dma((4,)), dma((4,)), dma, dma]
         + [dma((3, 4, 4))] * 2
         + [dma((3, 4))] * 2
-        + [dma((3, 3))] * 2
-        + [dma, dma],
+        + [dma((3, 4, 2))] * 2,
         compiler_params=pltpu.CompilerParams(
             collective_id=0, has_side_effects=True, vmem_limit_bytes=60 * 1024 * 1024
         ),

time: 102 us -> 98.4 us (0.965)
  Pallas kernels: 100 us -> 96.7 us
    pallas_call x1, Pallas kernels: 100 us -> 96.7 us  [per_device(): pl.pallas_call(block_kernel, out_shape=jax.ShapeDtypeStruct(tokens.shape,...]
where the time goes in v2:
time: 98.4 us; the launch traced here: 98.3 us
  Pallas kernels  96.7 us (98%)
  local copies, waits for them, and re-layouts  1.55 us (2%)
    pallas_call x1, Pallas kernels, per_device(): pl.pallas_call(block_kernel, out_shape=jax.ShapeDtypeStruct(tokens.shape,...  96.7 us

profile of v2, /device:TPU:1, one launch (start us, length us, event | category | flops | bytes accessed | tf_op | source)
XLA Modules:
  0.0 98.3 jit_solution(7747104635104485507)
XLA Ops:
  0.0 96.7 %gather_experts_sum.1 = bf16[8,7168]{1,0:T(8,128)(2,1)} custom-call(bf16[8,7168]{1,0:T(8,128)(2,1)} %tok.1, s32[2,8]{1,0:T(2,128)} %bitcast.18, s32[2,8]{1,0:T(2,128)} %bitcast.19, f32[1,7168]{1,0:T(1,128)} %bitcast.17, bf16[304,7168]{1,0:T(8,128)(2,1)} %bitcast.12, bf16[304,7168]{1,0:T(8,128)(2,1)} %bitcast.13, bf16[304,7168]{1,0:T(8,128)(2,1)} %bitcast.14, ...), custom_call_target="tpu_custom_call" | custom-call | tf_op jit(solution)/shard_map/gather_experts_sum/pallas_call | solution.py:459
  96.7 1.6 %copy.12 = bf16[8,7168]{1,0:T(8,128)(2,1)} copy(bf16[8,7168]{1,0:T(8,128)(2,1)} %gather_experts_sum.1) | data formatting | bytes 229376

commit v3 on v2

--- a/solution.py
+++ b/solution.py
@@ -81,7 +81,7 @@
     sibling = device(pos, rest)
     own_cols = pl.ds(pl.multiple_of(core * HALF, 128), HALF)
     rest_cols = pl.ds(pl.multiple_of(rest * HALF, 128), HALF)
-    x_low = lax.rem(pos[0], 2)
+    dense_x = (pos[0], 3 - pos[0])
     first = core == 0
     lower, upper = slice(0, 2), slice(2, 4)
     sends = []
@@ -94,6 +94,9 @@
         for copy in sends:
             copy.wait_send()
         sends.clear()
+
+    trades = [remote(he.at[x], he_in.at[x], he_s.at[x], he_r.at[x], sibling) for x in range(4)]
+    trade = remote(hd, hd_in, hd_s, hd_r, sibling)
 
     def gather(up_e, up_d, acc, acc_d):
         top, low = pl.ds(0, 304), pl.ds(304, 304)
@@ -190,7 +193,7 @@
             for h in range(2):
                 rows = jnp.concatenate(
                     [
-                        xs[j][h, x_low + 2 * k, :, pos[2]].reshape(64, xs[j].shape[-1])[:, : WIDTHS[j]]
+                        xs[j][h, dense_x[k], :, pos[2]].reshape(64, xs[j].shape[-1])[:, : WIDTHS[j]]
                         for k in range(2)
                     ],
                     axis=0,
@@ -235,9 +238,10 @@
                 copy(j, line(j, n, 0), g2s.at[j, k], g2r.at[j, k], sibling).wait_recv()
                 target = device(moved(pos, axis, d), core)
                 go(copy(j, line(j, n, 0, part), g2s.at[j, 2 + k], g2r.at[j, 2 + k], target))
-                own(j, n)
+            own(j, 1)
         for j in range(3):
             relay(j, 0)
+            own(j, 2)
         for j in range(3):
             for k, part in enumerate((lower, upper)):
                 copy(j, line(j, 3, 0, part), g2s.at[j, 2 + k], g2r.at[j, 2 + k], sibling).wait_recv()
@@ -270,35 +274,32 @@
         last(2)
         forwarded(2)
         adds(2, rest)
+        def glu(v):
+            g, u = v[:, :304], v[:, 304:]
+            return (g / (1.0 + jnp.exp(-g)) * u).astype(BF16)
+
         add_lines(3, core, (0, 1))
         forwarded(3, (0, 1))
         add_lines(3, rest, (0, 1))
         add_dense(0)
+        forwarded(3, (2,))
+        add_dense(1)
+        hd[...] = glu(acc_d[...])
+        trade.start()
         last(3)
         add_lines(3, core, (2, 3))
-        forwarded(3, (2, 3))
+        forwarded(3, (3,))
         add_lines(3, rest, (2, 3))
-
-        def glu(v):
-            g, u = v[:, :304], v[:, 304:]
-            return (g / (1.0 + jnp.exp(-g)) * u).astype(BF16)
 
         e = lax.axis_index("expert")
         lanes = lax.broadcasted_iota(jnp.int32, (256, 128), 1)
         pick = jnp.where(lanes == e, 32.0, 0.0) + jnp.where(lanes == e + 8, 1.0, 0.0)
-        trades = [remote(he.at[x], he_in.at[x], he_s.at[x], he_r.at[x], sibling) for x in range(4)]
         for x in range(4):
             he[x] = glu(acc[x].reshape(256, 608)).reshape(4, 4, 16, 304)
-            go(trades[x])
+            trades[x].start()
         for x in range(4):
             pieces = x2[core, x, :, :, :, WIDTHS[2] :].reshape(256, 128).astype(F32)
             weight[x] = (jnp.sum(pieces * pick, axis=1, keepdims=True) * (1.0 / 1024.0)).reshape(4, 4, 16, 1)
-        add_dense(1)
-        hd[...] = glu(acc_d[...])
-        go(remote(hd, hd_in, hd_s, hd_r, sibling))
-        for x in range(4):
-            trades[x].wait_recv()
-            heb[x] = jnp.concatenate([he[x].reshape(256, 304), he_in[x].reshape(256, 304)], axis=1).reshape(4, 4, 16, 608)
         for lend in lends:
             lend.wait_recv()
         settle()
@@ -322,12 +323,19 @@
             idx = where(j, step)
             axis = REDUCE[j][0]
             places = []
-            if axis == 0 and step % 2 == 0:
-                places = [((idx[0], ALL, pos[2]), (lax.div(idx[0], 2), ALL))]
+            if axis == 0 and step == 0:
+                places = [((idx[0], ALL, pos[2]), (0, ALL))]
             elif axis == 1:
-                places = [((x_low + 2 * k, idx[1], pos[2]), (k, idx[1])) for k in range(2)]
+                places = [((dense_x[k], idx[1], pos[2]), (k, idx[1])) for k in range(2)]
             elif axis == 2 and step == 0:
-                places = [((x_low + 2 * k, ALL, pos[2]), (k, ALL)) for k in range(2)]
+                places = [((dense_x[k], ALL, pos[2]), (k, ALL)) for k in range(2)]
+            elif axis == 0 and step % 2:
+
+                @pl.when(idx[0] == dense_x[1])
+                def _():
+                    spot = (idx[0], ALL, pos[2])
+                    zs[j][spot] = (zs[j][spot].astype(F32) + dense[j][1]).astype(BF16)
+
             for spot, src in places:
                 zs[j][spot] = (zs[j][spot].astype(F32) + dense[j][src]).astype(BF16)
 
@@ -363,41 +371,46 @@
             return (half2[j], full2[j], s2.at[j], r2.at[j])
 
         order = (2, 1, 3, 0)
-        def begin(j):
-            for i, r in enumerate(order):
-                bufs, _, ss, rr = outer(j, i)
-                halves(j, 2, r, REDUCE[j][0], bufs, ss, rr)
+        def begin(j, i):
+            bufs, _, ss, rr = outer(j, i)
+            halves(j, 2, order[i], REDUCE[j][0], bufs, ss, rr)
 
         def go_on(j, i, k):
             bufs, fulls, ss, rr = outer(j, i)
             whole(j, order[1 + k], order[i], REDUCE[j][0], k, bufs, fulls, ss, rr)
 
-        produce(2, 2)
-        begin(2)
-        remote(hd, hd_in, hd_s, hd_r, sibling).wait_recv()
+        trade.wait_recv()
         hdb[...] = jnp.concatenate([hd[...], hd_in[...]], axis=1)
         for j in range(3):
             part = dot(hdb[...], down_d[:, STARTS[j] : STARTS[j] + WIDTHS[j]])
             dense[j][...] = part.reshape(2, 4, 16, WIDTHS[j])
-            if j < 2:
-                produce(j, 2)
-                produce_dense(j, 2)
-                begin(j)
+        for x in range(4):
+            trades[x].wait_recv()
+            heb[x] = jnp.concatenate([he[x].reshape(256, 304), he_in[x].reshape(256, 304)], axis=1).reshape(4, 4, 16, 608)
+        for j in range(3):
+            produce(j, 2)
+            produce_dense(j, 2)
+            begin(j, 0)
+        def next_line(i):
+            for j in range(3):
+                for k in range(2):
+                    go_on(j, i, k)
+
         for k in range(2):
             for j in range(3):
                 produce(j, order[1 + k])
                 produce_dense(j, order[1 + k])
-            for i in range(3):
-                for j in range(3):
-                    go_on(j, i, k)
+                begin(j, 1 + k)
+        next_line(0)
+        for j in range(3):
+            begin(j, 3)
+        next_line(1)
         for j in range(3):
             produce(j, 0)
             produce_dense(j, 0)
         for i, r in enumerate(order):
-            if i == 2:
-                for j in range(3):
-                    for k in range(2):
-                        go_on(j, 3, k)
+            if i in (1, 2):
+                next_line(i + 1)
             for j in range(3):
                 _, fulls, ss, rr = outer(j, i)
                 close(j, r, fulls, ss, rr)
@@ -427,6 +440,8 @@
                     total = total + got[...].astype(F32)
                 cols = pl.ds(pl.multiple_of(half * HALF + STARTS[j], 128), WIDTHS[j])
                 out[:, cols] = (tok[:, cols].astype(F32) + total).astype(BF16)
+        for copy in (*trades, trade):
+            copy.wait_send()
         settle()
 
     wide = (608, tok.shape[1])

time: 98.4 us -> 97.7 us (level)
  no operation moved by 1% of the time
where the time goes in v3:
time: 97.7 us; the launch traced here: 97.6 us
  Pallas kernels  96 us (98%)
  local copies, waits for them, and re-layouts  1.55 us (2%)
    pallas_call x1, Pallas kernels, per_device(): pl.pallas_call(block_kernel, out_shape=jax.ShapeDtypeStruct(tokens.shape,...  96 us

profile of v3, /device:TPU:1, one launch (start us, length us, event | category | flops | bytes accessed | tf_op | source)
XLA Modules:
  0.0 97.6 jit_solution(1239681370429354374)
XLA Ops:
  0.0 96.0 %gather_experts_sum.1 = bf16[8,7168]{1,0:T(8,128)(2,1)} custom-call(bf16[8,7168]{1,0:T(8,128)(2,1)} %tok.1, s32[2,8]{1,0:T(2,128)} %bitcast.18, s32[2,8]{1,0:T(2,128)} %bitcast.19, f32[1,7168]{1,0:T(1,128)} %bitcast.17, bf16[304,7168]{1,0:T(8,128)(2,1)} %bitcast.12, bf16[304,7168]{1,0:T(8,128)(2,1)} %bitcast.13, bf16[304,7168]{1,0:T(8,128)(2,1)} %bitcast.14, ...), custom_call_target="tpu_custom_call" | custom-call | tf_op jit(solution)/shard_map/gather_experts_sum/pallas_call | solution.py:474
  96.0 1.6 %copy.12 = bf16[8,7168]{1,0:T(8,128)(2,1)} copy(bf16[8,7168]{1,0:T(8,128)(2,1)} %gather_experts_sum.1) | data formatting | bytes 229376

commit v4 on v3

--- a/solution.py
+++ b/solution.py
@@ -256,6 +256,9 @@
         forwarded(0)
         adds(0, rest)
         add_dense(2)
+        forwarded(1, (0,))
+        forwarded(2, (0,))
+        add_dense(0)
         for j in range(3):
             relay(j, 3)
         adds(1, core)
@@ -269,10 +272,10 @@
 
         last(0)
         last(1)
-        forwarded(1)
+        forwarded(1, (1, 2, 3))
         adds(1, rest)
         last(2)
-        forwarded(2)
+        forwarded(2, (1, 2, 3))
         adds(2, rest)
         def glu(v):
             g, u = v[:, :304], v[:, 304:]
@@ -281,7 +284,6 @@
         add_lines(3, core, (0, 1))
         forwarded(3, (0, 1))
         add_lines(3, rest, (0, 1))
-        add_dense(0)
         forwarded(3, (2,))
         add_dense(1)
         hd[...] = glu(acc_d[...])

time: 97.7 us -> 97.4 us (level)
  no operation moved by 1% of the time
where the time goes in v4:
time: 97.4 us; the launch traced here: 97.3 us
  Pallas kernels  95.7 us (98%)
  local copies, waits for them, and re-layouts  1.55 us (2%)
    pallas_call x1, Pallas kernels, per_device(): pl.pallas_call(block_kernel, out_shape=jax.ShapeDtypeStruct(tokens.shape,...  95.7 us

profile of v4, /device:TPU:1, one launch (start us, length us, event | category | flops | bytes accessed | tf_op | source)
XLA Modules:
  0.0 97.3 jit_solution(1185803227038848562)
XLA Ops:
  0.0 95.7 %gather_experts_sum.1 = bf16[8,7168]{1,0:T(8,128)(2,1)} custom-call(bf16[8,7168]{1,0:T(8,128)(2,1)} %tok.1, s32[2,8]{1,0:T(2,128)} %bitcast.18, s32[2,8]{1,0:T(2,128)} %bitcast.19, f32[1,7168]{1,0:T(1,128)} %bitcast.17, bf16[304,7168]{1,0:T(8,128)(2,1)} %bitcast.12, bf16[304,7168]{1,0:T(8,128)(2,1)} %bitcast.13, bf16[304,7168]{1,0:T(8,128)(2,1)} %bitcast.14, ...), custom_call_target="tpu_custom_call" | custom-call | tf_op jit(solution)/shard_map/gather_experts_sum/pallas_call | solution.py:476
  95.7 1.6 %copy.12 = bf16[8,7168]{1,0:T(8,128)(2,1)} copy(bf16[8,7168]{1,0:T(8,128)(2,1)} %gather_experts_sum.1) | data formatting | bytes 229376
